TPU v7x, 256 devices: a whole 4x4x8 slice. The times are simulated.
256 devices in a mesh: context: 64 (over x, z_hi, y, core), tensor: 4 (over z_lo).
Axes of the slice: x: 4, y: 4, z: 8 (z_hi: 2, z_lo: 4; z = z_hi * 4 + z_lo), core: 2. Of those that a mesh axis runs over, the one named last changes fastest.
Arguments:
- hidden_in: bfloat16 [32768, 4096], P(('context', 'tensor')), may hold values from -3 to 3
- norm_gain: float32 [4096], replicated, as said below
- w_query: bfloat16 [4096, 2048], P(None, 'tensor'), may hold values from -0.09375 to 0.09375
- w_key: bfloat16 [4096, 512], P(None, 'tensor'), may hold values from -0.09375 to 0.09375
- w_value: bfloat16 [4096, 512], P(None, 'tensor'), may hold values from -0.09375 to 0.09375
- w_out: bfloat16 [2048, 4096], P('tensor'), may hold values from -0.75 to 0.75
- offsets: int32 [64], replicated, may hold values from 0 to 127
Outputs:
- hidden_out: bfloat16 [32768, 4096], P(('context', 'tensor'))
Inputs may be any that keep to these rules, and one draw needn't show every extreme that they name: `norm_gain`: gains of order one, all positive.
All inputs are finite; a program needn't handle non-finite values.
Results may differ from a plain program's by a relative error of at most 0.025.
Values may be sent and summed in bfloat16 or wider, within the bound.
A program may use at most 64 MiB of HBM per device.

v0:
```python
import jax
import jax.numpy as jnp
from jax import lax
from jax.sharding import PartitionSpec as P

HD = 128


def spread(block, axis, source):
    block = jnp.where(lax.axis_index(axis) == source, block, jnp.zeros_like(block))
    return lax.psum(block, axis)


def rms_norm(rows_in, norm_gain):
    values = rows_in.astype(jnp.float32)
    mean_sq = jnp.mean(values * values, axis=-1, keepdims=True)
    return (values * lax.rsqrt(mean_sq + 1e-05) * norm_gain).astype(jnp.bfloat16)


def rope_apply(values, positions):
    half = values.shape[-1] // 2
    freq = 500000.0 ** (-(jnp.arange(half).astype(jnp.float32) * 2.0 / values.shape[-1]))
    angle = positions.astype(jnp.float32)[:, None] * freq[None, :]
    cosine = jnp.concatenate([jnp.cos(angle), jnp.cos(angle)], axis=-1)[:, None, :]
    sine = jnp.concatenate([jnp.sin(angle), jnp.sin(angle)], axis=-1)[:, None, :]
    turned = jnp.concatenate([-values[..., half:], values[..., :half]], axis=-1)
    return values * cosine + turned * sine


def body(hidden_in, norm_gain, w_query, w_key, w_value, w_out, offsets):
    query_cols = w_query.shape[1]
    key_cols = w_key.shape[1]
    normed = rms_norm(hidden_in, norm_gain)
    piece = lax.all_gather(normed, "tensor", axis=0, tiled=True)
    projected = jnp.concatenate(
        [
            jnp.dot(piece, w_query, preferred_element_type=jnp.float32),
            jnp.dot(piece, w_key, preferred_element_type=jnp.float32),
            jnp.dot(piece, w_value, preferred_element_type=jnp.float32),
        ],
        axis=1,
    )
    block_len = projected.shape[0]
    group = lax.axis_index("context")
    base_pos = jnp.arange(block_len)
    positions = offsets[group] * block_len + base_pos
    query = rope_apply(projected[:, :query_cols].reshape(block_len, -1, HD), positions).astype(
        jnp.bfloat16
    )
    own_key = rope_apply(
        projected[:, query_cols : query_cols + key_cols].reshape(block_len, -1, HD), positions
    ).astype(jnp.bfloat16)
    own_value = (
        projected[:, query_cols + key_cols :].astype(jnp.bfloat16).reshape(block_len, -1, HD)
    )
    anchor_states = spread(hidden_in, "context", 0)
    anchor_norm = rms_norm(anchor_states, norm_gain)
    piece = lax.all_gather(anchor_norm, "tensor", axis=0, tiled=True)
    anchor_proj = jnp.concatenate(
        [
            jnp.dot(piece, w_key, preferred_element_type=jnp.float32),
            jnp.dot(piece, w_value, preferred_element_type=jnp.float32),
        ],
        axis=1,
    )
    anchor_pos = offsets[0] * block_len + base_pos
    anchor_key = rope_apply(
        anchor_proj[:, :key_cols].reshape(block_len, -1, HD), anchor_pos
    ).astype(jnp.bfloat16)
    anchor_value = anchor_proj[:, key_cols:].astype(jnp.bfloat16).reshape(block_len, -1, HD)
    kv_local = own_key.shape[1]
    group_size = query.shape[1] // kv_local
    query_grouped = query.reshape(block_len, kv_local, group_size, HD)
    scale = 1.0 / HD**0.5
    neg = jnp.float32(-1e30)
    own_scores = (
        jnp.einsum("qkgd,skd->kgqs", query_grouped, own_key, preferred_element_type=jnp.float32)
        * scale
    )
    anchor_scores = (
        jnp.einsum("qkgd,skd->kgqs", query_grouped, anchor_key, preferred_element_type=jnp.float32)
        * scale
    )
    own_scores = jnp.where(base_pos[None, :] <= base_pos[:, None], own_scores, neg)
    anchor_scores = jnp.where(group == 0, neg, anchor_scores)
    scores = jnp.concatenate([anchor_scores, own_scores], axis=-1)
    top = jnp.max(scores, axis=-1, keepdims=True)
    expo = jnp.exp(scores - top)
    weights = (expo / jnp.sum(expo, axis=-1, keepdims=True)).astype(jnp.bfloat16)
    values_all = jnp.concatenate([anchor_value, own_value], axis=0)
    attended = jnp.einsum("kgqs,skd->qkgd", weights, values_all, preferred_element_type=jnp.float32)
    attended = attended.astype(jnp.bfloat16).reshape(block_len, query_cols)
    branch = lax.psum_scatter(
        jnp.dot(attended, w_out, preferred_element_type=jnp.float32).astype(jnp.bfloat16),
        "tensor",
        scatter_dimension=0,
        tiled=True,
    ).astype(jnp.float32)
    return (hidden_in.astype(jnp.float32) + branch).astype(jnp.bfloat16)


def solution(mesh):
    placed = (
        P(("context", "tensor"), None),
        P(),
        P(None, "tensor"),
        P(None, "tensor"),
        P(None, "tensor"),
        P("tensor", None),
        P(),
    )
    return jax.shard_map(
        body, mesh=mesh, in_specs=placed, out_specs=P(("context", "tensor"), None), check_vma=False
    )
```

profile of v0, /device:TPU:1, one launch (start us, length us, event | category | flops | bytes accessed | tf_op | source)
XLA Modules:
  0.0 1087.2 jit_solution(14562009865333965947)
XLA Ops:
  6.6 1.1 broadcast_select_fusion
  7.7 1.5 fusion.12
  9.2 787.2 %all-reduce.2.cloned.1.call-done = bf16[128,4096]{1,0:T(8,128)(2,1)} async-done(((bf16[128,4096]{1,0:T(8,128)(2,1)}), bf16[128,4096]{1,0:T(8,128)(2,1)}) %all-reduce.2.cloned.1.call-update) | async-done | bytes 1048592 | tf_op jit(solution)/shard_map/psum | solution.py:11
  796.5 1.5 fusion.9
  798.0 3.3 fusion.11
  801.4 0.7 all-gather.5.cloned.1.call-update
  802.1 0.6 fusion.41
  804.1 1.7 multiply_sine_fusion.1
  805.9 80.0 %all-gather.3.cloned.1.call-done = bf16[512,4096]{1,0:T(8,128)(2,1)} async-done(((bf16[128,4096]{1,0:T(8,128)(2,1)}), bf16[512,4096]{1,0:T(8,128)(2,1)}) %all-gather.3.cloned.1.call-update) | async-done | bytes 4194320 | tf_op jit(solution)/shard_map/all_gather | solution.py:58
  885.9 3.7 fusion.43
  889.6 0.7 fusion.31
  890.3 81.7 %all-gather.5.cloned.1.call-done = bf16[512,4096]{1,0:T(8,128)(2,1)} async-done(((bf16[128,4096]{1,0:T(8,128)(2,1)}), bf16[512,4096]{1,0:T(8,128)(2,1)}) %all-gather.5.cloned.1.call-update) | async-done | bytes 4194320 | tf_op jit(solution)/shard_map/all_gather | solution.py:34
  972.0 5.8 fusion.44
  977.9 0.1 slice_negate_fusion
  978.0 0.1 maximum_multiply_fusion
  978.1 0.3 fusion.21
  978.4 0.3 copy-done.5
  978.9 0.8 fusion.32
  979.6 0.6 fusion.7
  980.2 0.6 fusion.39
  980.8 1.6 copy-done.3
  982.4 1.5 fusion.45
  984.0 0.9 fusion.42
  984.9 1.2 fusion.3
  986.2 1.3 fusion.20
  987.4 0.9 copy-done.2
  988.4 1.3 fusion.19
  989.6 2.0 fusion.16
  991.7 0.1 copy-done.4
  991.8 4.4 convolution_convert_fusion
  996.2 82.0 %reduce-scatter.2.cloned.1.call-done = bf16[128,4096]{1,0:T(8,128)(2,1)} async-done(((bf16[512,4096]{1,0:T(8,128)(2,1)}), bf16[128,4096]{1,0:T(8,128)(2,1)}) %reduce-scatter.2.cloned.1.call-update) | async-done | bytes 1048592 | tf_op jit(solution)/shard_map/reduce_scatter | solution.py:93
  1078.3 2.4 fusion.15
  (34 shorter events, 0.6 us)
Async XLA Ops:
  6.5 879.3 %copy-start = (bf16[4096,128]{1,0:T(8,128)(2,1)S(1)}, bf16[4096,128]{1,0:T(8,128)(2,1)}, u32[]{:S(2)}) copy-start(bf16[4096,128]{1,0:T(8,128)(2,1)} %param.10) | copy-start | bytes 3145732
  6.5 791.4 %copy-start.1 = (bf16[128,4096]{1,0:T(8,128)(2,1)S(1)}, bf16[128,4096]{1,0:T(8,128)(2,1)}, u32[]{:S(2)}) copy-start(bf16[128,4096]{1,0:T(8,128)(2,1)} %param.7) | copy-start | bytes 3145732
  6.5 791.4 %copy-start.8 = (f32[4096]{0:T(1024)S(1)}, f32[4096]{0:T(1024)}, u32[]{:S(2)}) copy-start(f32[4096]{0:T(1024)} %param.8) | copy-start | bytes 49156
  6.5 789.9 %all-reduce.2.cloned.1.call-start = ((), (), s32[]{:S(2)}) async-start(), calls=%async_computation.1 | async-start | bytes 2097152 | tf_op jit(solution)/shard_map/psum | solution.py:11
  7.6 794.5 %copy-start.9 = (s32[64]{0:T(128)S(1)}, s32[64]{0:T(128)}, u32[]{:S(2)}) copy-start(s32[64]{0:T(128)} %param.13) | copy-start | bytes 772
  7.6 878.2 %all-gather.3.cloned.1.call-start = ((), (), s32[]{:S(2)}) async-start(), calls=%async_computation.2 | async-start | bytes 5242880 | tf_op jit(solution)/shard_map/all_gather | solution.py:58
  801.3 170.7 %all-gather.5.cloned.1.call-start = ((), (), s32[]{:S(2)}) async-start(), calls=%async_computation.3 | async-start | bytes 5242880 | tf_op jit(solution)/shard_map/all_gather | solution.py:34
  802.0 276.2 %reduce-scatter.2.cloned.1.call-start = ((), (), s32[]{:S(2)}) async-start(), calls=%async_computation.4 | async-start | bytes 5242880 | tf_op jit(solution)/shard_map/reduce_scatter | solution.py:93
  977.8 0.9 copy-start.5
  977.8 1.0 copy-start.6
  977.9 1.0 copy-start.7
  980.2 2.2 copy-start.3
  984.9 1.2 copy-start.10
  986.2 2.2 copy-start.2
  989.6 2.2 copy-start.4
Sparse Core Ops, SparseCore 0:
  10.0 786.4 all-reduce.1
  801.4 84.3 all-gather.2
  887.8 84.1 all-gather.4
  996.3 81.8 reduce-scatter.1
where the time goes:
time: 1090 us
  waiting for transfers between devices  1030 us (94%)
  matrix products  21.7 us (2%)
  other arithmetic  15.3 us (1%)
  between operations  14.6 us (1%)
    psum x1, waiting for transfers between devices, spread(): return lax.psum(block, axis)  787 us
    reduce_scatter x1, waiting for transfers between devices, body(): lax.psum_scatter(jnp.dot(attended, w_out, preferred_element_type=jnp.floa...  82 us
    all_gather x1, waiting for transfers between devices, body(): piece = lax.all_gather(normed, 'tensor', axis=0, tiled=True)  81.7 us
    all_gather x1, waiting for transfers between devices, body(): piece = lax.all_gather(anchor_norm, 'tensor', axis=0, tiled=True)  80 us
  transfers between devices with their start and end apart: 4, of which 4 were waited for; matrix products, arithmetic and copies ran while one was open for 1% of the time, Pallas kernels for 0%

commit v1 on v0

v1 whole, which is shorter than its diff:
```python
import functools

import jax
import jax.numpy as jnp
from jax import lax
from jax.experimental import pallas as pl
from jax.experimental.pallas import tpu as pltpu
from jax.sharding import PartitionSpec as P

HD = 128
EPS = 1e-05
NEG = -1e30
MESH = pl.DeviceIdType.MESH
F32 = jnp.float32
BF16 = jnp.bfloat16
N_SEM = 96


def kernel(
    x_ref, gain_ref, cos_ref, sin_ref, wq_hbm, wk_hbm, wv_hbm, wo_hbm, out_ref,
    w_q, w_kv, w_o, normed, grain, grain_norm, anchor_kv, own_kv, q_buf, att, send_buf, recv_buf, partial,
    ss, rs, ls,
):
    ctx = lax.axis_index("context")
    t = lax.axis_index("tensor")
    core = ctx % 2
    y = (ctx // 2) % 4
    zh = (ctx // 8) % 2
    x = ctx // 16
    a = x * (1 - core) + y * core
    b = y * (1 - core) + x * core
    m = b * 4 + a
    mine = core * 16 + m
    slot = t // 2
    other = 1 - slot
    parity = t % 2

    def at(x_, y_, zh_, t_, core_):
        return (((x_ * 2 + zh_) * 4 + y_) * 2 + core_, t_)

    def ring_a(d):
        return at((x + d * (1 - core)) % 4, (y + d * core) % 4, zh, t, core)

    def ring_b(d):
        return at((x + d * core) % 4, (y + d * (1 - core)) % 4, zh, t, core)

    sibling = at(x, y, zh, t, 1 - core)
    pair = at(x, y, zh, t + 1 - 2 * parity, core)
    outer = (t // 2 + t) % 2
    wpart = at(x, y, (zh + 1 - outer) % 2, 3 - t, core)
    mirror = at(x, y, zh, 3 - t, core)
    same_type = [at(x, y, 1 - zh, t, core), at(x, y, zh, 3 - t, core), at(x, y, 1 - zh, 3 - t, core)]

    count = [0]
    sends = []

    def sem():
        count[0] += 1
        return count[0] - 1

    def send(k, src, dst, dev, keep=True):
        cp = pltpu.make_async_remote_copy(
            src_ref=src, dst_ref=dst, send_sem=ss.at[k], recv_sem=rs.at[k], device_id=dev, device_id_type=MESH
        )
        cp.start()
        if keep:
            sends.append(cp)
        return cp

    def recv(k, dst, dev):
        pltpu.make_async_remote_copy(
            src_ref=dst, dst_ref=dst, send_sem=ss.at[k], recv_sem=rs.at[k], device_id=dev, device_id_type=MESH
        ).wait_recv()

    is_source = ctx == 0
    takes = (zh == 0) & (core == slot)
    takes_first = takes & (m // 8 == parity)
    takes_second = takes & (m // 8 != parity)
    self_grain = is_source & (t == 0)

    bar = pltpu.get_barrier_semaphore()
    peers = [ring_a(d) for d in (1, 2, 3)] + [ring_b(d) for d in (1, 2, 3)] + [sibling, pair] + same_type
    for p in peers:
        pl.semaphore_signal(bar, inc=1, device_id=p, device_id_type=MESH)

    @pl.when(takes_first & jnp.logical_not(self_grain))
    def _():
        pl.semaphore_signal(bar, inc=1, device_id=(0, t), device_id_type=MESH)

    loads = []
    for i, (src, dst) in enumerate(
        [
            (wk_hbm, w_kv.at[slot, :, pl.ds(0, 128)]),
            (wv_hbm, w_kv.at[slot, :, pl.ds(128, 128)]),
            (wq_hbm, w_q.at[slot]),
            (wo_hbm, w_o.at[slot]),
        ]
    ):
        cp = pltpu.make_async_copy(src, dst, ls.at[i])
        cp.start()
        loads.append(cp)

    grains_out = jnp.where(is_source, jnp.where(t == 0, 7, 8), 0)
    pl.semaphore_wait(bar, len(peers) + grains_out)

    k_scat = [sem() for _ in range(8)]

    def grain_target(j):
        mm = 8 * parity + j
        aa = mm % 4
        bb = mm // 4
        return at(aa * (1 - slot) + bb * slot, bb * (1 - slot) + aa * slot, 0, t, slot)

    def grain_copy(j):
        return pltpu.make_async_remote_copy(
            src_ref=x_ref.at[pl.ds(16 * j, 16)], dst_ref=grain, send_sem=ss.at[k_scat[j]], recv_sem=rs.at[k_scat[0]],
            device_id=grain_target(j), device_id_type=MESH,
        )

    @pl.when(is_source)
    def _():
        for j in range(1, 8):
            grain_copy(j).start()

    @pl.when(is_source & (t != 0))
    def _():
        grain_copy(0).start()

    @pl.when(self_grain)
    def _():
        cp = pltpu.make_async_copy(x_ref.at[pl.ds(0, 16)], grain, ls.at[4])
        cp.start()
        cp.wait()

    def kv_view(start, n):
        return w_kv.at[other, pl.ds(pl.multiple_of(start * 128, 128), n * 128)]

    def q_view(start, n):
        return w_q.at[other, pl.ds(pl.multiple_of(start * 128, 128), n * 128)]

    def o_view(start, n):
        return w_o.at[other, pl.ds(pl.multiple_of(start * 16, 16), n * 16)]

    def anchor_view(start, n):
        return anchor_kv.at[:, pl.ds(pl.multiple_of(start * 16, 16), n * 16)]

    rows128 = pl.ds(pl.multiple_of(mine * 128, 128), 128)
    rows16 = pl.ds(pl.multiple_of(mine * 16, 16), 16)
    k_zk, k_zv, k_zq, k_zo = sem(), sem(), sem(), sem()
    send(k_zk, wk_hbm.at[rows128], w_kv.at[slot, rows128, pl.ds(0, 128)], wpart)
    send(k_zv, wv_hbm.at[rows128], w_kv.at[slot, rows128, pl.ds(128, 128)], wpart)
    send(k_zq, wq_hbm.at[rows128], w_q.at[slot, rows128], wpart)
    send(k_zo, wo_hbm.at[rows16], w_o.at[slot, rows16], wpart)

    class Gather:
        def __init__(self, view):
            self.view = view
            self.ka = [sem() for _ in range(3)]
            self.kb = [sem() for _ in range(3)]
            self.kd = [sem() for _ in range(4)]

        def send_a(self):
            v = self.view(mine, 1)
            for d in (1, 3, 2):
                send(self.ka[d - 1], v, v, ring_a(d))

        def wait_a(self):
            for d in (1, 3, 2):
                recv(self.ka[d - 1], self.view(core * 16 + b * 4 + (a + 4 - d) % 4, 1), ring_a(4 - d))

        def send_b(self):
            v = self.view(core * 16 + b * 4, 4)
            for d in (1, 3, 2):
                send(self.kb[d - 1], v, v, ring_b(d))
            send(self.kd[0], v, v, sibling)

        def wait_b(self):
            for d in (1, 3, 2):
                v = self.view(core * 16 + ((b + 4 - d) % 4) * 4, 4)
                recv(self.kb[d - 1], v, ring_b(4 - d))
                send(self.kd[d], v, v, sibling)

        def wait_d(self):
            for d in (0, 1, 3, 2):
                recv(self.kd[d], self.view((1 - core) * 16 + ((a + 4 - d) % 4) * 4, 4), sibling)

    kv_gather, q_gather, o_gather, an_gather = (Gather(v) for v in (kv_view, q_view, o_view, anchor_view))

    def norm(rows):
        v = rows.astype(F32)
        mean_sq = jnp.mean(v * v, axis=-1, keepdims=True)
        return (v * lax.rsqrt(mean_sq + EPS) * gain_ref[...]).astype(BF16)

    my_half = parity
    k_norm = [sem() for _ in range(4)]

    for i in range(4):

        @pl.loop(0, 2)
        def _(r, i=i):
            rr = pl.ds(pl.multiple_of(i * 32 + r * 16, 16), 16)
            normed[my_half, rr] = norm(x_ref[rr])

        v = normed.at[my_half, pl.ds(i * 32, 32)]
        send(k_norm[i], v, v, pair)

    recv(k_zk, w_kv.at[other, rows128, pl.ds(0, 128)], wpart)
    recv(k_zv, w_kv.at[other, rows128, pl.ds(128, 128)], wpart)
    kv_gather.send_a()

    k_pair = sem()

    def grain_forward():
        return pltpu.make_async_remote_copy(
            src_ref=grain, dst_ref=grain, send_sem=ss.at[k_pair], recv_sem=rs.at[k_pair], device_id=pair, device_id_type=MESH
        )

    @pl.when(takes_first & jnp.logical_not(self_grain))
    def _():
        recv(k_scat[0], grain, (0, t))

    @pl.when(takes_first)
    def _():
        grain_forward().start()

    kv_gather.wait_a()
    kv_gather.send_b()
    recv(k_zq, w_q.at[other, rows128], wpart)
    q_gather.send_a()
    kv_gather.wait_b()
    q_gather.wait_a()
    q_gather.send_b()
    recv(k_zo, w_o.at[other, rows16], wpart)
    o_gather.send_a()
    for cp in loads:
        cp.wait()
    kv_gather.wait_d()

    def rope(v, c, s):
        return v * c + pltpu.roll(v, 64, 1) * s

    k_an = [sem() for _ in range(3)]
    an_mine = anchor_view(mine, 1)

    def anchor_copy(i):
        return pltpu.make_async_remote_copy(
            src_ref=an_mine, dst_ref=an_mine, send_sem=ss.at[k_an[i]], recv_sem=rs.at[k_an[0]],
            device_id=same_type[i], device_id_type=MESH,
        )

    @pl.when(takes_second)
    def _():
        recv(k_pair, grain, pair)

    @pl.when(takes)
    def _():
        grain_norm[...] = norm(grain[...])
        c = cos_ref[pl.ds(256, 16)]
        s = sin_ref[pl.ds(256, 16)]
        for i in range(2):
            kv = jnp.dot(grain_norm[...], w_kv[i], preferred_element_type=F32)
            anchor_kv[i, rows16, pl.ds(0, 128)] = rope(kv[:, :128], c, s).astype(BF16)
            anchor_kv[i, rows16, pl.ds(128, 128)] = kv[:, 128:].astype(BF16)
        for i in range(3):
            anchor_copy(i).start()

    def kv_rows(half, start, n):
        rows = pl.ds(start, n)
        table = pl.ds(pl.multiple_of(half * 128 + start, 16), n)
        c = cos_ref[table]
        s = sin_ref[table]
        place = pl.ds(pl.multiple_of((slot * 2 + half) * 128 + start, 16), n)
        for i in range(2):
            kv = jnp.dot(normed[half, rows], w_kv[i], preferred_element_type=F32)
            own_kv[i, place, pl.ds(0, 128)] = rope(kv[:, :128], c, s).astype(BF16)
            own_kv[i, place, pl.ds(128, 128)] = kv[:, 128:].astype(BF16)

    k_kv = [sem() for _ in range(5)]

    def kv_copy(k, half, start, n):
        v = own_kv.at[:, pl.ds(pl.multiple_of(half * 128 + start, 16), n)]
        return pltpu.make_async_remote_copy(
            src_ref=v, dst_ref=v, send_sem=ss.at[k], recv_sem=rs.at[k], device_id=mirror, device_id_type=MESH
        )

    kv_rows(my_half, 0, 128)
    lower = slot == 0

    @pl.when(lower)
    def _():
        kv_copy(k_kv[0], my_half, 0, 128).start()
        own_kv[:, pl.ds(256, 256)] = jnp.zeros((2, 256, 256), BF16)

    @pl.when(jnp.logical_not(takes))
    def _():
        recv(k_an[0], an_mine, pair)

    an_gather.send_a()

    def q_rows(half, i):
        table = pl.ds(pl.multiple_of(half * 128, 128), 128)

        @pl.loop(0, 2)
        def _(j):
            c = cos_ref[table]
            s = sin_ref[table]
            q = jnp.dot(
                normed[half], w_q[i, :, pl.ds(pl.multiple_of(j * 256, 256), 256)], preferred_element_type=F32
            )
            for h in range(2):
                q_buf[half, i, j * 2 + h] = rope(q[:, h * 128 : (h + 1) * 128], c, s).astype(BF16)

    q_rows(my_half, slot)
    an_gather.wait_a()
    an_gather.send_b()
    q_gather.wait_b()
    o_gather.wait_a()
    o_gather.send_b()
    an_gather.wait_b()
    q_gather.wait_d()
    q_rows(my_half, other)

    far = 1 - my_half
    for i in range(4):
        recv(k_norm[i], normed.at[far, pl.ds(i * 32, 32)], pair)
        kv_rows(far, i * 32, 32)

        @pl.when(lower)
        def _(i=i):
            kv_copy(k_kv[1 + i], far, i * 32, 32).start()

    q_rows(far, slot)
    q_rows(far, other)
    an_gather.wait_d()
    o_gather.wait_b()

    @pl.when(jnp.logical_not(lower))
    def _():
        kv_copy(k_kv[0], 1 - my_half, 0, 128).wait_recv()
        for i in range(4):
            kv_copy(k_kv[1 + i], my_half, i * 32, 32).wait_recv()

    scale = 1.0 / HD**0.5
    first_group = ctx == 0

    def attend(half):
        @pl.loop(0, 8)
        def _(h):
            i = h // 4
            q = q_buf[half, i, h % 4]
            dims = (((1,), (1,)), ((), ()))
            s1 = lax.dot_general(q, anchor_kv[i, :, pl.ds(0, 128)], dims, preferred_element_type=F32)
            s2 = lax.dot_general(q, own_kv[i, :, pl.ds(0, 128)], dims, preferred_element_type=F32)
            qpos = (slot * 2 + half) * 128 + lax.broadcasted_iota(jnp.int32, (128, 512), 0)
            kpos = lax.broadcasted_iota(jnp.int32, (128, 512), 1)
            s1 = jnp.where(first_group, NEG, s1 * scale)
            s2 = jnp.where(kpos <= qpos, s2 * scale, NEG)
            top = jnp.maximum(jnp.max(s1, axis=-1, keepdims=True), jnp.max(s2, axis=-1, keepdims=True))
            e1 = jnp.exp(s1 - top)
            e2 = jnp.exp(s2 - top)
            total = jnp.sum(e1, axis=-1, keepdims=True) + jnp.sum(e2, axis=-1, keepdims=True)
            o = jnp.dot(e1.astype(BF16), anchor_kv[i, :, pl.ds(128, 128)], preferred_element_type=F32)
            o += jnp.dot(e2.astype(BF16), own_kv[i, :, pl.ds(128, 128)], preferred_element_type=F32)
            att[half, i, :, pl.ds(pl.multiple_of((h % 4) * 128, 128), 128)] = (o / total).astype(BF16)

    def out_cols(half, start, n):
        cols = pl.ds(pl.multiple_of(start, 256), n)
        return jnp.dot(att[half, 0], w_o[0, :, cols], preferred_element_type=F32) + jnp.dot(
            att[half, 1], w_o[1, :, cols], preferred_element_type=F32
        )

    attend(far)
    o_gather.wait_d()
    k_sum = [sem() for _ in range(4)]
    for i in range(4):

        @pl.loop(0, 4)
        def _(j, i=i):
            send_buf[i, :, pl.ds(pl.multiple_of(j * 256, 256), 256)] = out_cols(far, i * 1024 + j * 256, 256).astype(BF16)

        send(k_sum[i], send_buf.at[i], recv_buf.at[i], pair)

    attend(my_half)

    @pl.loop(0, 16)
    def _(j):
        cols = pl.ds(pl.multiple_of(j * 256, 256), 256)
        partial[:, cols] = x_ref[:, cols].astype(F32) + out_cols(my_half, j * 256, 256)

    @pl.when(is_source)
    def _():
        for j in range(1, 8):
            grain_copy(j).wait_send()

    @pl.when(is_source & (t != 0))
    def _():
        grain_copy(0).wait_send()

    @pl.when(takes_first)
    def _():
        grain_forward().wait_send()

    @pl.when(takes)
    def _():
        for i in range(3):
            anchor_copy(i).wait_send()

    @pl.when(lower)
    def _():
        kv_copy(k_kv[0], my_half, 0, 128).wait_send()
        for i in range(4):
            kv_copy(k_kv[1 + i], far, i * 32, 32).wait_send()

    for cp in sends[:-4]:
        cp.wait_send()
    for i in range(4):
        recv(k_sum[i], recv_buf.at[i], pair)

        @pl.loop(0, 4)
        def _(j, i=i):
            cols = pl.ds(pl.multiple_of(i * 1024 + j * 256, 256), 256)
            got = recv_buf[i, :, pl.ds(pl.multiple_of(j * 256, 256), 256)].astype(F32)
            out_ref[:, cols] = (partial[:, cols] + got).astype(BF16)

    for cp in sends[-4:]:
        cp.wait_send()
    assert count[0] <= N_SEM, count[0]


def tables(offsets):
    ctx = lax.axis_index("context")
    t = lax.axis_index("tensor")
    core = ctx % 2
    y = (ctx // 2) % 4
    x = ctx // 16
    a = x * (1 - core) + y * core
    b = y * (1 - core) + x * core
    rows = jnp.arange(272)
    own = offsets[ctx] * 512 + (t // 2) * 256 + rows
    anchor = offsets[0] * 512 + (core * 16 + b * 4 + a) * 16 + rows - 256
    positions = jnp.where(rows < 256, own, anchor).astype(F32)
    half = HD // 2
    freq = 500000.0 ** (-(jnp.arange(half).astype(F32) * 2.0 / HD))
    angle = positions[:, None] * freq[None, :]
    c = jnp.cos(angle)
    s = jnp.sin(angle)
    return jnp.concatenate([c, c], axis=-1), jnp.concatenate([-s, s], axis=-1)


def body(hidden_in, norm_gain, w_query, w_key, w_value, w_out, offsets):
    cosine, sine = tables(offsets)
    vmem = pl.BlockSpec(memory_space=pltpu.VMEM)
    hbm = pl.BlockSpec(memory_space=pl.ANY)
    return pl.pallas_call(
        kernel,
        out_shape=jax.ShapeDtypeStruct((128, 4096), BF16),
        in_specs=[vmem] * 4 + [hbm] * 4,
        out_specs=vmem,
        scratch_shapes=[
            pltpu.VMEM((2, 4096, 512), BF16),
            pltpu.VMEM((2, 4096, 256), BF16),
            pltpu.VMEM((2, 512, 4096), BF16),
            pltpu.VMEM((2, 128, 4096), BF16),
            pltpu.VMEM((16, 4096), BF16),
            pltpu.VMEM((16, 4096), BF16),
            pltpu.VMEM((2, 512, 256), BF16),
            pltpu.VMEM((2, 512, 256), BF16),
            pltpu.VMEM((2, 2, 4, 128, 128), BF16),
            pltpu.VMEM((2, 2, 128, 512), BF16),
            pltpu.VMEM((4, 128, 1024), BF16),
            pltpu.VMEM((4, 128, 1024), BF16),
            pltpu.VMEM((128, 4096), F32),
            pltpu.SemaphoreType.DMA((N_SEM,)),
            pltpu.SemaphoreType.DMA((N_SEM,)),
            pltpu.SemaphoreType.DMA((5,)),
        ],
        compiler_params=pltpu.CompilerParams(collective_id=0, has_side_effects=True, vmem_limit_bytes=56 * 2**20),
        cost_estimate=pl.CostEstimate(flops=10**10, bytes_accessed=2 * 10**7, transcendentals=2 * 10**6),
    )(hidden_in, norm_gain.reshape(1, 4096), cosine, sine, w_query, w_key, w_value, w_out)


def solution(mesh):
    placed = (
        P(("context", "tensor"), None),
        P(),
        P(None, "tensor"),
        P(None, "tensor"),
        P(None, "tensor"),
        P("tensor", None),
        P(),
    )
    return jax.shard_map(
        body, mesh=mesh, in_specs=placed, out_specs=P(("context", "tensor"), None), check_vma=False
    )
```

time: 1090 us -> 98.2 us (0.09)
  waiting for transfers between devices: 1030 us -> 0 us
  Pallas kernels: 0 us -> 91.7 us
  matrix products: 21.7 us -> 0 us
  other arithmetic: 15.3 us -> 1.42 us
  between operations: 14.6 us -> 1.32 us
    psum x1 -> x0, waiting for transfers between devices: 787 us -> none  [spread(): return lax.psum(block, axis)]
    all_gather x2 -> x0, waiting for transfers between devices: 162 us -> none  [the longest x1 81.7 us: body(): piece = lax.all_gather(normed, 'tensor', axis=0, tiled=True)]
    pallas_call x0 -> x1, Pallas kernels: none -> 91.7 us  [body(): pl.pallas_call(kernel, out_shape=jax.ShapeDtypeStruct((128, 4096), BF16),...]
    reduce_scatter x1 -> x0, waiting for transfers between devices: 82 us -> none  [body(): lax.psum_scatter(jnp.dot(attended, w_out, preferred_element_type=jnp.floa...]
    dot_general x9 -> x0, matrix products: 21.7 us -> none  [the longest x1 5.83 us: body(): jnp.dot(piece, w_query, preferred_element_type=jnp.float32)]
  transfers between devices with their start and end apart: 4 -> 0, of which waited for: 4 -> 0; matrix products, arithmetic and copies ran while one was open for 1% -> 0% of each run, Pallas kernels for 0% -> 0%
where the time goes in v1:
time: 98.2 us; the launch traced here: 98 us
  Pallas kernels  91.7 us (93%)
  local copies, waits for them, and re-layouts  3.61 us (4%)
  other arithmetic  1.42 us (1%)
  between operations  1.32 us (1%)
    pallas_call x1, Pallas kernels, body(): pl.pallas_call(kernel, out_shape=jax.ShapeDtypeStruct((128, 4096), BF16),...  91.7 us
    unnamed x1, local copies, waits for them, and re-layouts  2.29 us

profile of v1, /device:TPU:1, one launch (start us, length us, event | category | flops | bytes accessed | tf_op | source)
XLA Modules:
  0.0 98.0 jit_solution(5964447189824646789)
XLA Ops:
  0.0 1.3 %fusion.1 = (s32[1]{0:T(128)}, s32[1]{0:T(128)}) fusion(s32[64]{0:T(128)} %param.13, s32[]{:T(128)S(6)} %select_n.32), kind=kLoop, calls=%fused_computation.8 | loop fusion | bytes 20 | tf_op jit(solution)/shard_map/dynamic_slice | solution.py:439
  2.6 0.6 fusion
  3.2 0.8 pad_maximum_fusion
  4.0 91.7 %shard_map.73 = bf16[128,4096]{1,0:T(8,128)(2,1)} custom-call(bf16[128,4096]{1,0:T(8,128)(2,1)} %x_ref.1, f32[1,4096]{1,0:T(1,128)} %bitcast.3, f32[272,128]{1,0:T(8,128)} %get-tuple-element.10.cos_ref, f32[272,128]{1,0:T(8,128)} %get-tuple-element.11.sin_ref, bf16[4096,512]{1,0:T(8,128)(2,1)} %wq_hbm.1, bf16[4096,128]{1,0:T(8,128)(2,1)} %wk_hbm.1, ...), custom_call_target="tpu_custom_call" | custom-call | flops 10000000000 | bytes 20000000 | tf_op jit(solution)/shard_map/pallas_call | solution.py:454
  95.7 2.3 %copy.9 = bf16[128,4096]{1,0:T(8,128)(2,1)} copy(bf16[128,4096]{1,0:T(8,128)(2,1)} %shard_map.73) | data formatting | bytes 2097152
  (2 shorter events, 0.0 us)

commit v2 on v1

v2 whole, which is shorter than its diff:
```python
import jax
import jax.numpy as jnp
import numpy as np
from jax import lax
from jax.experimental import pallas as pl
from jax.experimental.pallas import tpu as pltpu
from jax.sharding import PartitionSpec as P

HD = 128
EPS = 1e-05
NEG = -1e30
MESH = pl.DeviceIdType.MESH
F32 = jnp.float32
BF16 = jnp.bfloat16
N_SEM = 144


def kernel(
    offsets_ref, x_ref, gain_ref, base_cos, base_sin, row_cos, row_sin, wq_hbm, wk_hbm, wv_hbm, wo_hbm, out_ref,
    w_q, w_kv, w_o, normed, grain, grain_norm, anchor_kv, block_kv, q_own, q_near, att_own, att_near, send_buf, recv_buf,
    partial, cos_ref, sin_ref, ss, rs, ls,
):
    ctx = lax.axis_index("context")
    t = lax.axis_index("tensor")
    core = ctx % 2
    y = (ctx // 2) % 4
    zh = (ctx // 8) % 2
    x = ctx // 16
    a = x * (1 - core) + y * core
    b = y * (1 - core) + x * core
    m = b * 4 + a
    mine = core * 16 + m
    slot = t // 2
    other = 1 - slot
    parity = t % 2

    def at(x_, y_, zh_, t_, core_):
        return (((x_ * 2 + zh_) * 4 + y_) * 2 + core_, t_)

    def ring_a(d):
        return at((x + d * (1 - core)) % 4, (y + d * core) % 4, zh, t, core)

    def ring_b(d):
        return at((x + d * core) % 4, (y + d * (1 - core)) % 4, zh, t, core)

    def along_z(d):
        z = (zh * 4 + t + d) % 8
        return at(x, y, z // 4, z % 4, core)

    sibling = at(x, y, zh, t, 1 - core)
    above, below = along_z(1), along_z(7)
    pair = at(x, y, zh, t + 1 - 2 * parity, core)
    wpart = at(x, y, (zh + core) % 2, (t + 2) % 4, core)
    same_type = [along_z(2), along_z(4), along_z(6)]
    foreign = ctx + 8 - 16 * zh
    low_foreign = jnp.where(t == 0, 1, 0)
    high_foreign = jnp.where(t == 3, 1, 0)
    low_ctx = ctx + (foreign - ctx) * low_foreign
    high_ctx = ctx + (foreign - ctx) * high_foreign
    own_start = t * 128
    low_start = (t * 128 + 448) % 512
    high_start = (t * 128 + 128) % 512

    count = [0]
    sends = []

    def sem():
        count[0] += 1
        return count[0] - 1

    def send(k, src, dst, dev, keep=True):
        cp = pltpu.make_async_remote_copy(
            src_ref=src, dst_ref=dst, send_sem=ss.at[k], recv_sem=rs.at[k], device_id=dev, device_id_type=MESH
        )
        cp.start()
        if keep:
            sends.append(cp)
        return cp

    def recv(k, dst, dev):
        pltpu.make_async_remote_copy(
            src_ref=dst, dst_ref=dst, send_sem=ss.at[k], recv_sem=rs.at[k], device_id=dev, device_id_type=MESH
        ).wait_recv()

    is_source = ctx == 0
    takes = (zh == 0) & (core == slot)
    takes_first = takes & (m // 8 == parity)
    takes_second = takes & (m // 8 != parity)
    self_grain = is_source & (t == 0)

    bar = pltpu.get_barrier_semaphore()
    peers = [ring_a(d) for d in (1, 2, 3)] + [ring_b(d) for d in (1, 2, 3)] + [sibling, above, below] + same_type
    for p in peers:
        pl.semaphore_signal(bar, inc=1, device_id=p, device_id_type=MESH)

    @pl.when(takes_first & jnp.logical_not(self_grain))
    def _():
        pl.semaphore_signal(bar, inc=1, device_id=(0, t), device_id_type=MESH)

    loads = []
    for i, (src, dst) in enumerate(
        [
            (wk_hbm, w_kv.at[slot, :, pl.ds(0, 128)]),
            (wv_hbm, w_kv.at[slot, :, pl.ds(128, 128)]),
        ]
        + [(wq_hbm.at[pl.ds(j * 512, 512)], w_q.at[slot, j]) for j in range(8)]
        + [(wo_hbm.at[:, pl.ds(j * 512, 512)], w_o.at[slot, j]) for j in range(8)]
    ):
        cp = pltpu.make_async_copy(src, dst, ls.at[i])
        cp.start()
        loads.append(cp)

    def fill_tables(at_row, n, row, offset):
        cb = base_cos[pl.ds(offset, 1)]
        sb = base_sin[pl.ds(offset, 1)]
        cr = row_cos[pl.ds(row, n)]
        sr = row_sin[pl.ds(row, n)]
        cos_ref[pl.ds(at_row, n)] = cb * cr - sb * sr
        sin_ref[pl.ds(at_row, n)] = sb * cr + cb * sr

    fill_tables(0, 128, pl.multiple_of(own_start, 128), offsets_ref[ctx])
    fill_tables(128, 64, pl.multiple_of(low_start, 64), offsets_ref[low_ctx])
    fill_tables(192, 64, pl.multiple_of(high_start, 64), offsets_ref[high_ctx])
    fill_tables(256, 16, pl.multiple_of(mine * 16, 16), offsets_ref[0])

    grains_out = jnp.where(is_source, jnp.where(t == 0, 7, 8), 0)
    pl.semaphore_wait(bar, len(peers) + grains_out)

    rows128 = pl.ds(pl.multiple_of(mine * 128, 128), 128)
    rows16 = pl.ds(pl.multiple_of(mine * 16, 16), 16)
    my_block = core * 4 + b
    o_cols = pl.ds(pl.multiple_of(my_block * 512, 512), 512)
    quarter = pl.ds(pl.multiple_of(a * 128, 128), 128)
    k_zk, k_zv, k_zq, k_zo = sem(), sem(), sem(), sem()
    send(k_zk, wk_hbm.at[rows128], w_kv.at[slot, rows128, pl.ds(0, 128)], wpart)
    send(k_zv, wv_hbm.at[rows128], w_kv.at[slot, rows128, pl.ds(128, 128)], wpart)
    send(k_zq, wq_hbm.at[rows128], w_q.at[slot, my_block, quarter], wpart)

    k_scat = [sem() for _ in range(8)]

    def grain_target(j):
        mm = 8 * parity + j
        aa = mm % 4
        bb = mm // 4
        return at(aa * (1 - slot) + bb * slot, bb * (1 - slot) + aa * slot, 0, t, slot)

    def grain_copy(j):
        return pltpu.make_async_remote_copy(
            src_ref=x_ref.at[pl.ds(16 * j, 16)], dst_ref=grain, send_sem=ss.at[k_scat[j]], recv_sem=rs.at[k_scat[0]],
            device_id=grain_target(j), device_id_type=MESH,
        )

    @pl.when(is_source)
    def _():
        for j in range(1, 8):
            grain_copy(j).start()

    @pl.when(is_source & (t != 0))
    def _():
        grain_copy(0).start()

    @pl.when(self_grain)
    def _():
        cp = pltpu.make_async_copy(x_ref.at[pl.ds(0, 16)], grain, ls.at[18])
        cp.start()
        cp.wait()

    def kv_one(c_, b_, a_):
        return w_kv.at[other, pl.ds(pl.multiple_of((c_ * 16 + b_ * 4 + a_) * 128, 128), 128)]

    def kv_block(c_, b_):
        return w_kv.at[other, pl.ds(pl.multiple_of((c_ * 4 + b_) * 512, 512), 512)]

    def an_one(c_, b_, a_):
        return anchor_kv.at[:, pl.ds(pl.multiple_of((c_ * 16 + b_ * 4 + a_) * 16, 16), 16)]

    def an_block(c_, b_):
        return anchor_kv.at[:, pl.ds(pl.multiple_of((c_ * 4 + b_) * 64, 64), 64)]

    class Gather:
        def __init__(self, one, block):
            self.one, self.block = one, block
            self.ka = [sem() for _ in range(3)]
            self.kb = [sem() for _ in range(3)]
            self.kd = [sem() for _ in range(4)]

        def send_a(self):
            v = self.one(core, b, a)
            for d in (1, 3, 2):
                send(self.ka[d - 1], v, v, ring_a(d))

        def wait_a(self):
            for d in (1, 3, 2):
                recv(self.ka[d - 1], self.one(core, b, (a + 4 - d) % 4), ring_a(4 - d))

        def send_b(self):
            v = self.block(core, b)
            for d in (1, 3, 2):
                send(self.kb[d - 1], v, v, ring_b(d))
            send(self.kd[0], v, v, sibling)

        def wait_b(self):
            for d in (1, 3, 2):
                v = self.block(core, (b + 4 - d) % 4)
                recv(self.kb[d - 1], v, ring_b(4 - d))
                send(self.kd[d], v, v, sibling)

        def wait_d(self):
            for d in (0, 1, 3, 2):
                recv(self.kd[d], self.block(1 - core, (a + 4 - d) % 4), sibling)

    class Stream:
        def __init__(self, block, pieces, slices):
            self.block, self.n, self.g = block, pieces, 512 // pieces
            self.ka = [sem() for _ in range(3)] if slices else []
            self.kb = [[sem() for _ in range(2)] for _ in range(pieces)]
            self.kc = [[sem() for _ in range(2)] for _ in range(pieces)]
            self.kd = [[sem() for _ in range(4)] for _ in range(pieces)]

        def piece(self, c_, b_, k):
            return self.block(c_, b_, pl.ds(k * self.g, self.g))

        def half(self, b_, k, h):
            return self.block(core, b_, pl.ds(k * self.g + h * (self.g // 2), self.g // 2))

        def one(self, a_):
            return self.block(core, b, pl.ds(pl.multiple_of(a_ * 128, 128), 128))

        def send_a(self):
            v = self.one(a)
            for d in (1, 3, 2):
                send(self.ka[d - 1], v, v, ring_a(d))

        def wait_a(self):
            for d in (1, 3, 2):
                recv(self.ka[d - 1], self.one((a + 4 - d) % 4), ring_a(4 - d))

        def first(self, k):
            v = self.piece(core, b, k)
            for i, d in enumerate((1, 3)):
                send(self.kb[k][i], v, v, ring_b(d))
            send(self.kd[k][0], v, v, sibling)

        def on(self, k):
            for i, d in enumerate((1, 3)):
                near = (b + 4 - d) % 4
                recv(self.kb[k][i], self.piece(core, near, k), ring_b(4 - d))
                v = self.half(near, k, i)
                send(self.kc[k][i], v, v, ring_b(d))
                v = self.piece(core, near, k)
                send(self.kd[k][d], v, v, sibling)

        def last(self, k):
            far_b = (b + 2) % 4
            for i, d in enumerate((1, 3)):
                recv(self.kc[k][i], self.half(far_b, k, i), ring_b(4 - d))
            v = self.piece(core, far_b, k)
            send(self.kd[k][2], v, v, sibling)

        def wait_d(self, ds=(0, 1, 3, 2)):
            for d in ds:
                for k in range(self.n):
                    recv(self.kd[k][d], self.piece(1 - core, (a + 4 - d) % 4, k), sibling)

    def q_view(c_, b_, rows):
        return w_q.at[other, c_ * 4 + b_, rows]

    def o_view(c_, b_, rows):
        return w_o.at[other, c_ * 4 + b_, rows]

    kv_gather = Gather(kv_one, kv_block)
    an_gather = Gather(an_one, an_block)
    q_str = Stream(q_view, 2, True)
    o_str = Stream(o_view, 2, True)

    def norm(rows):
        v = rows.astype(F32)
        mean_sq = jnp.mean(v * v, axis=-1, keepdims=True)
        return (v * lax.rsqrt(mean_sq + EPS) * gain_ref[...]).astype(BF16)

    k_norm = [sem() for _ in range(2)]
    for i in range(2):

        @pl.loop(0, 4)
        def _(r, i=i):
            rr = pl.ds(pl.multiple_of(i * 64 + r * 16, 16), 16)
            normed[rr] = norm(x_ref[rr])

        if i == 0:
            send(k_norm[0], normed.at[pl.ds(0, 64)], normed.at[pl.ds(192, 64)], below)
        else:
            send(k_norm[1], normed.at[pl.ds(64, 64)], normed.at[pl.ds(128, 64)], above)

    recv(k_zk, w_kv.at[other, rows128, pl.ds(0, 128)], wpart)
    recv(k_zv, w_kv.at[other, rows128, pl.ds(128, 128)], wpart)
    kv_gather.send_a()

    k_pair = sem()

    def grain_forward():
        return pltpu.make_async_remote_copy(
            src_ref=grain, dst_ref=grain, send_sem=ss.at[k_pair], recv_sem=rs.at[k_pair], device_id=pair, device_id_type=MESH
        )

    @pl.when(takes_first & jnp.logical_not(self_grain))
    def _():
        recv(k_scat[0], grain, (0, t))

    @pl.when(takes_first)
    def _():
        grain_forward().start()

    recv(k_zq, q_str.one(a), wpart)
    q_str.send_a()
    kv_gather.wait_a()
    kv_gather.send_b()
    send(k_zo, wo_hbm.at[quarter, o_cols], w_o.at[slot, my_block, quarter], wpart)
    for cp in loads:
        cp.wait()

    def rope(v, c, s):
        return v * c + pltpu.roll(v, 64, 1) * s

    k_own = [sem() for _ in range(4)]
    k_low, k_high, k_high4 = sem(), sem(), sem()

    def kv_view(buf, i, start, n):
        return block_kv.at[buf, i, pl.ds(pl.multiple_of(start, 64), n)]

    def kv_send(k, src, dst, dev):
        return pltpu.make_async_remote_copy(
            src_ref=src, dst_ref=dst, send_sem=ss.at[k], recv_sem=rs.at[k], device_id=dev, device_id_type=MESH
        )

    both = pl.ds(0, 2)
    to_foreign = jnp.where(t == 2, 1, 0)

    def own_to_2(n, i):
        return kv_send(k_own[n], kv_view(0, i, own_start, 128), kv_view(to_foreign, i, own_start, 128), along_z(2))

    def own_to_4(n, i):
        return kv_send(k_own[2 + n], kv_view(0, i, 0, 128), kv_view(1, i, 0, 128), along_z(4))

    def low_to_2():
        return kv_send(k_low, kv_view(0, both, low_start, 64), kv_view(to_foreign, both, low_start, 64), along_z(2))

    def high_to_2():
        return kv_send(
            k_high, kv_view(high_foreign, both, high_start, 64), kv_view(to_foreign, both, high_start, 64), along_z(2)
        )

    def high_to_4():
        return kv_send(
            k_high4, kv_view(high_foreign, both, high_start, 64), kv_view(low_foreign, both, high_start, 64), along_z(4)
        )

    def kv_own(n, i):
        kv = jnp.dot(normed[pl.ds(0, 128)], w_kv[i], preferred_element_type=F32)
        rows = pl.ds(pl.multiple_of(own_start, 128), 128)
        block_kv[0, i, rows, pl.ds(0, 128)] = rope(kv[:, :128], cos_ref[pl.ds(0, 128)], sin_ref[pl.ds(0, 128)]).astype(BF16)
        block_kv[0, i, rows, pl.ds(128, 128)] = kv[:, 128:].astype(BF16)

        @pl.when(t <= 2)
        def _():
            own_to_2(n, i).start()

        @pl.when(t == 0)
        def _():
            own_to_4(n, i).start()

    def kv_near():
        for i in range(2):
            kv = jnp.dot(normed[pl.ds(128, 128)], w_kv[i], preferred_element_type=F32)
            key = rope(kv[:, :128], cos_ref[pl.ds(128, 128)], sin_ref[pl.ds(128, 128)]).astype(BF16)
            value = kv[:, 128:].astype(BF16)
            low_rows = pl.ds(pl.multiple_of(low_start, 64), 64)
            high_rows = pl.ds(pl.multiple_of(high_start, 64), 64)
            block_kv[low_foreign, i, low_rows, pl.ds(0, 128)] = key[:64]
            block_kv[low_foreign, i, low_rows, pl.ds(128, 128)] = value[:64]
            block_kv[high_foreign, i, high_rows, pl.ds(0, 128)] = key[64:]
            block_kv[high_foreign, i, high_rows, pl.ds(128, 128)] = value[64:]
        high_to_2().start()

        @pl.when((t == 1) | (t == 2))
        def _():
            low_to_2().start()

        @pl.when((t == 0) | (t == 3))
        def _():
            high_to_4().start()

    for n in range(4):

        @pl.when(t == n)
        def _(n=n):
            if n < 3:
                start = n * 128 + 192
                block_kv[0, :, pl.ds(start, 512 - start)] = jnp.zeros((2, 512 - start, 256), BF16)
            else:
                block_kv[1, :, pl.ds(64, 448)] = jnp.zeros((2, 448, 256), BF16)

    kv_own(0, slot)

    def q_rows(near, i):
        rows = pl.ds(near * 128, 128)

        @pl.loop(0, 2)
        def _(j):
            c = cos_ref[rows]
            s = sin_ref[rows]
            q = jnp.dot(
                normed[rows], w_q[i, :, :, pl.ds(pl.multiple_of(j * 256, 256), 256)].reshape(4096, 256),
                preferred_element_type=F32,
            )
            for h in range(2):
                v = rope(q[:, h * 128 : (h + 1) * 128], c, s).astype(BF16)
                if near:
                    place = pl.ds(pl.multiple_of((j * 2 + h) * 64, 64), 64)
                    q_near[i, 0, place] = v[:64]
                    q_near[i, 1, place] = v[64:]
                else:
                    q_own[i, j, pl.ds(h * 128, 128)] = v

    q_rows(0, slot)
    q_str.wait_a()
    q_str.first(0)
    q_str.first(1)
    kv_gather.wait_b()

    @pl.when(takes_second)
    def _():
        recv(k_pair, grain, pair)

    @pl.when(takes)
    def _():
        grain_norm[...] = norm(grain[...])

    kv_gather.wait_d()

    k_an = [sem() for _ in range(3)]
    an_mine = an_one(core, b, a)

    def anchor_copy(i):
        return pltpu.make_async_remote_copy(
            src_ref=an_mine, dst_ref=an_mine, send_sem=ss.at[k_an[i]], recv_sem=rs.at[k_an[0]],
            device_id=same_type[i], device_id_type=MESH,
        )

    @pl.when(takes)
    def _():
        c = cos_ref[pl.ds(256, 16)]
        s = sin_ref[pl.ds(256, 16)]
        for i in range(2):
            kv = jnp.dot(grain_norm[...], w_kv[i], preferred_element_type=F32)
            anchor_kv[i, rows16, pl.ds(0, 128)] = rope(kv[:, :128], c, s).astype(BF16)
            anchor_kv[i, rows16, pl.ds(128, 128)] = kv[:, 128:].astype(BF16)
        for i in range(3):
            anchor_copy(i).start()

    kv_own(1, other)
    recv(k_zo, o_str.one(a), wpart)
    o_str.send_a()
    recv(k_norm[0], normed.at[pl.ds(192, 64)], above)
    recv(k_norm[1], normed.at[pl.ds(128, 64)], below)
    kv_near()

    @pl.when(jnp.logical_not(takes))
    def _():
        recv(k_an[0], an_mine, pair)

    an_gather.send_a()
    q_rows(1, slot)
    q_str.on(0)
    q_str.on(1)
    an_gather.wait_a()
    an_gather.send_b()
    o_str.wait_a()
    o_str.first(0)
    o_str.first(1)
    q_str.last(0)
    q_str.last(1)
    an_gather.wait_b()
    q_str.wait_d()
    q_rows(1, other)
    an_gather.wait_d()

    @pl.when(t != 1)
    def _():
        for n in range(2):
            v = kv_view(low_foreign, n, (own_start + 256) % 512, 128)
            kv_send(k_own[n], v, v, along_z(6)).wait_recv()

    @pl.when((t == 0) | (t == 3))
    def _():
        v = kv_view(low_foreign, both, (low_start + 256) % 512, 64)
        kv_send(k_low, v, v, along_z(6)).wait_recv()
        v = kv_view(low_foreign, both, high_start, 64)
        kv_send(k_high4, v, v, along_z(4)).wait_recv()

    @pl.when(t == 0)
    def _():
        for n in range(2):
            v = kv_view(1, n, 0, 128)
            kv_send(k_own[2 + n], v, v, along_z(4)).wait_recv()

    v = kv_view(low_foreign, both, (high_start + 256) % 512, 64)
    recv(k_high, v, along_z(6))

    scale = 1.0 / HD**0.5
    dims = (((1,), (1,)), ((), ()))

    def attend(q, i, buf, block, start, length):
        s1 = lax.dot_general(q, anchor_kv[i, :, pl.ds(0, 128)], dims, preferred_element_type=F32)
        s2 = lax.dot_general(q, block_kv[buf, i, :, pl.ds(0, 128)], dims, preferred_element_type=F32)
        qpos = start + lax.broadcasted_iota(jnp.int32, (256, 512), 0) % length
        kpos = lax.broadcasted_iota(jnp.int32, (256, 512), 1)
        s1 = jnp.where(block == 0, NEG, s1 * scale)
        s2 = jnp.where(kpos <= qpos, s2 * scale, NEG)
        top = jnp.maximum(jnp.max(s1, axis=-1, keepdims=True), jnp.max(s2, axis=-1, keepdims=True))
        e1 = jnp.exp(s1 - top)
        e2 = jnp.exp(s2 - top)
        total = jnp.sum(e1, axis=-1, keepdims=True) + jnp.sum(e2, axis=-1, keepdims=True)
        o = jnp.dot(e1.astype(BF16), anchor_kv[i, :, pl.ds(128, 128)], preferred_element_type=F32)
        o += jnp.dot(e2.astype(BF16), block_kv[buf, i, :, pl.ds(128, 128)], preferred_element_type=F32)
        return (o / total).astype(BF16)

    @pl.loop(0, 2)
    def _(i):
        o = attend(q_near[i, 0], i, low_foreign, low_ctx, low_start, 64)
        for h in range(4):
            att_near[i, pl.ds(0, 64), pl.ds(h * 128, 128)] = o[h * 64 : (h + 1) * 64]
        o = attend(q_near[i, 1], i, high_foreign, high_ctx, high_start, 64)
        for h in range(4):
            att_near[i, pl.ds(64, 64), pl.ds(h * 128, 128)] = o[h * 64 : (h + 1) * 64]

    order = [core * 4 + b, (1 - core) * 4 + a]
    order += [core * 4 + (b + 3) % 4, core * 4 + (b + 1) % 4, (1 - core) * 4 + (a + 3) % 4, (1 - core) * 4 + (a + 1) % 4]
    order += [core * 4 + (b + 2) % 4, (1 - core) * 4 + (a + 2) % 4]
    k_sum = [(sem(), sem()) for _ in range(8)]
    lower, upper = pl.ds(0, 64), pl.ds(64, 64)

    def out_block(att, j):
        return jnp.dot(att[0], w_o[0, j], preferred_element_type=F32) + jnp.dot(att[1], w_o[1, j], preferred_element_type=F32)

    def send_sum(i):
        send_buf[i] = out_block(att_near, order[i]).astype(BF16)
        send(k_sum[i][0], send_buf.at[i, lower], recv_buf.at[i, upper], below)
        send(k_sum[i][1], send_buf.at[i, upper], recv_buf.at[i, lower], above)

    send_sum(0)
    o_str.wait_d((0,))
    send_sum(1)
    o_str.on(0)
    o_str.on(1)
    send_sum(2)
    send_sum(3)
    o_str.wait_d((1, 3))
    send_sum(4)
    send_sum(5)
    o_str.last(0)
    o_str.last(1)
    send_sum(6)
    o_str.wait_d((2,))
    send_sum(7)
    q_rows(0, other)

    @pl.loop(0, 4)
    def _(n):
        i = n // 2
        o = attend(q_own[i, n % 2], i, 0, ctx, own_start, 128)
        for h in range(2):
            att_own[i, :, pl.ds(pl.multiple_of((n % 2) * 256 + h * 128, 128), 128)] = o[h * 128 : (h + 1) * 128]

    @pl.loop(0, 8)
    def _(j):
        cols = pl.ds(pl.multiple_of(j * 512, 512), 512)
        partial[:, cols] = x_ref[:, cols].astype(F32) + out_block(att_own, j)

    @pl.when(is_source)
    def _():
        for j in range(1, 8):
            grain_copy(j).wait_send()

    @pl.when(is_source & (t != 0))
    def _():
        grain_copy(0).wait_send()

    @pl.when(takes_first)
    def _():
        grain_forward().wait_send()

    @pl.when(takes)
    def _():
        for i in range(3):
            anchor_copy(i).wait_send()

    @pl.when(t <= 2)
    def _():
        for n in range(2):
            own_to_2(n, n).wait_send()

    @pl.when(t == 0)
    def _():
        for n in range(2):
            own_to_4(n, n).wait_send()

    high_to_2().wait_send()

    @pl.when((t == 1) | (t == 2))
    def _():
        low_to_2().wait_send()

    @pl.when((t == 0) | (t == 3))
    def _():
        high_to_4().wait_send()

    for cp in sends[:-16]:
        cp.wait_send()
    for i in range(8):
        recv(k_sum[i][0], recv_buf.at[i, upper], above)
        recv(k_sum[i][1], recv_buf.at[i, lower], below)
        cols = pl.ds(pl.multiple_of(order[i] * 512, 512), 512)
        out_ref[:, cols] = (partial[:, cols] + recv_buf[i].astype(F32)).astype(BF16)
    for cp in sends[-16:]:
        cp.wait_send()
    assert count[0] <= N_SEM, count[0]


def angle_tables():
    freq = 500000.0 ** (-(np.arange(HD // 2) * 2.0 / HD))
    sign = np.concatenate([-np.ones(HD // 2), np.ones(HD // 2)])[None]

    def both(positions):
        angle = np.asarray(positions, np.float64)[:, None] * np.concatenate([freq, freq])[None]
        return np.cos(angle).astype(np.float32), (np.sin(angle) * sign).astype(np.float32)

    return (*both(np.arange(128) * 512), *both(np.arange(512)))


def body(hidden_in, norm_gain, w_query, w_key, w_value, w_out, offsets):
    vmem = pl.BlockSpec(memory_space=pltpu.VMEM)
    hbm = pl.BlockSpec(memory_space=pl.ANY)
    return pl.pallas_call(
        kernel,
        out_shape=jax.ShapeDtypeStruct((128, 4096), BF16),
        in_specs=[pl.BlockSpec(memory_space=pltpu.SMEM)] + [vmem] * 6 + [hbm] * 4,
        out_specs=vmem,
        scratch_shapes=[
            pltpu.VMEM((2, 8, 512, 512), BF16),
            pltpu.VMEM((2, 4096, 256), BF16),
            pltpu.VMEM((2, 8, 512, 512), BF16),
            pltpu.VMEM((256, 4096), BF16),
            pltpu.VMEM((16, 4096), BF16),
            pltpu.VMEM((16, 4096), BF16),
            pltpu.VMEM((2, 512, 256), BF16),
            pltpu.VMEM((2, 2, 512, 256), BF16),
            pltpu.VMEM((2, 2, 256, 128), BF16),
            pltpu.VMEM((2, 2, 256, 128), BF16),
            pltpu.VMEM((2, 128, 512), BF16),
            pltpu.VMEM((2, 128, 512), BF16),
            pltpu.VMEM((8, 128, 512), BF16),
            pltpu.VMEM((8, 128, 512), BF16),
            pltpu.VMEM((128, 4096), F32),
            pltpu.VMEM((272, 128), F32),
            pltpu.VMEM((272, 128), F32),
            pltpu.SemaphoreType.DMA((N_SEM,)),
            pltpu.SemaphoreType.DMA((N_SEM,)),
            pltpu.SemaphoreType.DMA((19,)),
        ],
        compiler_params=pltpu.CompilerParams(collective_id=0, has_side_effects=True, vmem_limit_bytes=56 * 2**20),
        cost_estimate=pl.CostEstimate(flops=10**10, bytes_accessed=2 * 10**7, transcendentals=2 * 10**6),
    )(offsets, hidden_in, norm_gain.reshape(1, 4096), *angle_tables(), w_query, w_key, w_value, w_out)


def solution(mesh):
    placed = (
        P(("context", "tensor"), None),
        P(),
        P(None, "tensor"),
        P(None, "tensor"),
        P(None, "tensor"),
        P("tensor", None),
        P(),
    )
    return jax.shard_map(
        body, mesh=mesh, in_specs=placed, out_specs=P(("context", "tensor"), None), check_vma=False
    )
```

time: 98.2 us -> 80 us (0.81)
  Pallas kernels: 91.7 us -> 77.5 us
  other arithmetic: 1.42 us -> 0 us
  local copies, waits for them, and re-layouts: 3.61 us -> 2.29 us
  between operations: 1.32 us -> 0.01 us
    pallas_call x1, Pallas kernels: 91.7 us -> 77.5 us  [body(): pl.pallas_call(kernel, out_shape=jax.ShapeDtypeStruct((128, 4096), BF16),...]
    dynamic_slice x1 -> x0, local copies, waits for them, and re-layouts: 1.32 us -> none  [tables(): own = offsets[ctx] * 512 + t // 2 * 256 + rows]
where the time goes in v2:
time: 80 us; the launch traced here: 79.8 us
  Pallas kernels  77.5 us (97%)
  local copies, waits for them, and re-layouts  2.29 us (3%)
    pallas_call x1, Pallas kernels, body(): pl.pallas_call(kernel, out_shape=jax.ShapeDtypeStruct((128, 4096), BF16),...  77.5 us
    unnamed x1, local copies, waits for them, and re-layouts  2.29 us

profile of v2, /device:TPU:1, one launch (start us, length us, event | category | flops | bytes accessed | tf_op | source)
XLA Modules:
  0.0 79.8 jit_solution(17829859992616420066)
XLA Ops:
  0.0 77.5 %shard_map.109 = bf16[128,4096]{1,0:T(8,128)(2,1)} custom-call(s32[64]{0:T(128)} %offsets_ref.1, bf16[128,4096]{1,0:T(8,128)(2,1)} %x_ref.1, f32[1,4096]{1,0:T(1,128)} %bitcast.1, f32[128,128]{1,0:T(8,128)} %constant.8.clone.base_cos, f32[128,128]{1,0:T(8,128)} %constant.9.clone.base_sin, f32[512,128]{1,0:T(8,128)} %constant.10.clone.row_cos, ...), custom_call_target="tpu_custom_call" | custom-call | flops 10000000000 | bytes 20000000 | tf_op jit(solution)/shard_map/pallas_call | solution.py:643
  77.6 2.3 %copy.13 = bf16[128,4096]{1,0:T(8,128)(2,1)} copy(bf16[128,4096]{1,0:T(8,128)(2,1)} %shard_map.109) | data formatting | bytes 2097152

commit v3 on v2

--- a/solution.py
+++ b/solution.py
@@ -16,9 +16,9 @@
 
 
 def kernel(
-    offsets_ref, x_ref, gain_ref, base_cos, base_sin, row_cos, row_sin, wq_hbm, wk_hbm, wv_hbm, wo_hbm, out_ref,
+    offsets_ref, gain_ref, x_hbm, tables_hbm, wq_hbm, wk_hbm, wv_hbm, wo_hbm, out_ref,
     w_q, w_kv, w_o, normed, grain, grain_norm, anchor_kv, block_kv, q_own, q_near, att_own, att_near, send_buf, recv_buf,
-    partial, cos_ref, sin_ref, ss, rs, ls,
+    partial, cos_ref, sin_ref, x_ref, tables_ref, ss, rs, ls,
 ):
     ctx = lax.axis_index("context")
     t = lax.axis_index("tensor")
@@ -90,6 +90,10 @@
 
     bar = pltpu.get_barrier_semaphore()
     peers = [ring_a(d) for d in (1, 2, 3)] + [ring_b(d) for d in (1, 2, 3)] + [sibling, above, below] + same_type
+    for d in (1, 2, 3):
+        for dz in (2, 4, 6):
+            z = (zh * 4 + t + dz) % 8
+            peers.append(at((x + d * (1 - core)) % 4, (y + d * core) % 4, z // 4, z % 4, core))
     for p in peers:
         pl.semaphore_signal(bar, inc=1, device_id=p, device_id_type=MESH)
 
@@ -97,6 +101,10 @@
     def _():
         pl.semaphore_signal(bar, inc=1, device_id=(0, t), device_id_type=MESH)
 
+    x_load = pltpu.make_async_copy(x_hbm, x_ref, ls.at[19])
+    x_load.start()
+    table_load = pltpu.make_async_copy(tables_hbm, tables_ref, ls.at[20])
+    table_load.start()
     loads = []
     for i, (src, dst) in enumerate(
         [
@@ -111,17 +119,12 @@
         loads.append(cp)
 
     def fill_tables(at_row, n, row, offset):
-        cb = base_cos[pl.ds(offset, 1)]
-        sb = base_sin[pl.ds(offset, 1)]
-        cr = row_cos[pl.ds(row, n)]
-        sr = row_sin[pl.ds(row, n)]
+        cb = tables_ref[0, pl.ds(512 + offset, 1)]
+        sb = tables_ref[1, pl.ds(512 + offset, 1)]
+        cr = tables_ref[0, pl.ds(row, n)]
+        sr = tables_ref[1, pl.ds(row, n)]
         cos_ref[pl.ds(at_row, n)] = cb * cr - sb * sr
         sin_ref[pl.ds(at_row, n)] = sb * cr + cb * sr
-
-    fill_tables(0, 128, pl.multiple_of(own_start, 128), offsets_ref[ctx])
-    fill_tables(128, 64, pl.multiple_of(low_start, 64), offsets_ref[low_ctx])
-    fill_tables(192, 64, pl.multiple_of(high_start, 64), offsets_ref[high_ctx])
-    fill_tables(256, 16, pl.multiple_of(mine * 16, 16), offsets_ref[0])
 
     grains_out = jnp.where(is_source, jnp.where(t == 0, 7, 8), 0)
     pl.semaphore_wait(bar, len(peers) + grains_out)
@@ -135,7 +138,9 @@
     send(k_zk, wk_hbm.at[rows128], w_kv.at[slot, rows128, pl.ds(0, 128)], wpart)
     send(k_zv, wv_hbm.at[rows128], w_kv.at[slot, rows128, pl.ds(128, 128)], wpart)
     send(k_zq, wq_hbm.at[rows128], w_q.at[slot, my_block, quarter], wpart)
-
+    send(k_zo, wo_hbm.at[quarter, o_cols], w_o.at[slot, my_block, quarter], wpart)
+
+    x_load.wait()
     k_scat = [sem() for _ in range(8)]
 
     def grain_target(j):
@@ -180,7 +185,7 @@
     class Gather:
         def __init__(self, one, block):
             self.one, self.block = one, block
-            self.ka = [sem() for _ in range(3)]
+            self.ka = [sem() for _ in range(3)] if one else []
             self.kb = [sem() for _ in range(3)]
             self.kd = [sem() for _ in range(4)]
 
@@ -269,8 +274,8 @@
         return w_o.at[other, c_ * 4 + b_, rows]
 
     kv_gather = Gather(kv_one, kv_block)
-    an_gather = Gather(an_one, an_block)
-    q_str = Stream(q_view, 2, True)
+    an_gather = Gather(None, an_block)
+    q_str = Stream(q_view, 4, True)
     o_str = Stream(o_view, 2, True)
 
     def norm(rows):
@@ -278,7 +283,7 @@
         mean_sq = jnp.mean(v * v, axis=-1, keepdims=True)
         return (v * lax.rsqrt(mean_sq + EPS) * gain_ref[...]).astype(BF16)
 
-    k_norm = [sem() for _ in range(2)]
+    k_norm = [sem() for _ in range(4)]
     for i in range(2):
 
         @pl.loop(0, 4)
@@ -287,9 +292,9 @@
             normed[rr] = norm(x_ref[rr])
 
         if i == 0:
-            send(k_norm[0], normed.at[pl.ds(0, 64)], normed.at[pl.ds(192, 64)], below)
+            send(k_norm[0], normed.at[pl.ds(0, 32)], normed.at[pl.ds(192, 32)], below)
         else:
-            send(k_norm[1], normed.at[pl.ds(64, 64)], normed.at[pl.ds(128, 64)], above)
+            send(k_norm[1], normed.at[pl.ds(64, 32)], normed.at[pl.ds(128, 32)], above)
 
     recv(k_zk, w_kv.at[other, rows128, pl.ds(0, 128)], wpart)
     recv(k_zv, w_kv.at[other, rows128, pl.ds(128, 128)], wpart)
@@ -310,11 +315,20 @@
     def _():
         grain_forward().start()
 
+    send(k_norm[2], normed.at[pl.ds(32, 32)], normed.at[pl.ds(224, 32)], below)
+    send(k_norm[3], normed.at[pl.ds(96, 32)], normed.at[pl.ds(160, 32)], above)
+
     recv(k_zq, q_str.one(a), wpart)
     q_str.send_a()
     kv_gather.wait_a()
     kv_gather.send_b()
-    send(k_zo, wo_hbm.at[quarter, o_cols], w_o.at[slot, my_block, quarter], wpart)
+    recv(k_zo, o_str.one(a), wpart)
+    o_str.send_a()
+    table_load.wait()
+    fill_tables(0, 128, pl.multiple_of(own_start, 128), offsets_ref[ctx])
+    fill_tables(128, 64, pl.multiple_of(low_start, 64), offsets_ref[low_ctx])
+    fill_tables(192, 64, pl.multiple_of(high_start, 64), offsets_ref[high_ctx])
+    fill_tables(256, 16, pl.multiple_of(mine * 16, 16), offsets_ref[0])
     for cp in loads:
         cp.wait()
 
@@ -425,6 +439,8 @@
     q_str.wait_a()
     q_str.first(0)
     q_str.first(1)
+    q_str.first(2)
+    q_str.first(3)
     kv_gather.wait_b()
 
     @pl.when(takes_second)
@@ -437,13 +453,18 @@
 
     kv_gather.wait_d()
 
-    k_an = [sem() for _ in range(3)]
+    k_an = [sem() for _ in range(15)]
+    k_an_in = [sem() for _ in range(4)]
     an_mine = an_one(core, b, a)
-
-    def anchor_copy(i):
+    zs, ds = (0, 2, 4, 6), (0, 1, 3, 2)
+
+    def anchor_copy(n):
+        dz, d = [(i, j) for j in ds for i in zs][1:][n]
+        z = (zh * 4 + t + dz) % 8
+        dev = at((x + d * (1 - core)) % 4, (y + d * core) % 4, z // 4, z % 4, core)
         return pltpu.make_async_remote_copy(
-            src_ref=an_mine, dst_ref=an_mine, send_sem=ss.at[k_an[i]], recv_sem=rs.at[k_an[0]],
-            device_id=same_type[i], device_id_type=MESH,
+            src_ref=an_mine, dst_ref=an_mine, send_sem=ss.at[k_an[n]], recv_sem=rs.at[k_an_in[d]],
+            device_id=dev, device_id_type=MESH,
         )
 
     @pl.when(takes)
@@ -454,34 +475,41 @@
             kv = jnp.dot(grain_norm[...], w_kv[i], preferred_element_type=F32)
             anchor_kv[i, rows16, pl.ds(0, 128)] = rope(kv[:, :128], c, s).astype(BF16)
             anchor_kv[i, rows16, pl.ds(128, 128)] = kv[:, 128:].astype(BF16)
-        for i in range(3):
+        for i in range(15):
             anchor_copy(i).start()
 
     kv_own(1, other)
-    recv(k_zo, o_str.one(a), wpart)
-    o_str.send_a()
-    recv(k_norm[0], normed.at[pl.ds(192, 64)], above)
-    recv(k_norm[1], normed.at[pl.ds(128, 64)], below)
-    kv_near()
-
-    @pl.when(jnp.logical_not(takes))
-    def _():
-        recv(k_an[0], an_mine, pair)
-
-    an_gather.send_a()
-    q_rows(1, slot)
     q_str.on(0)
     q_str.on(1)
-    an_gather.wait_a()
-    an_gather.send_b()
+    recv(k_norm[0], normed.at[pl.ds(192, 32)], above)
+    recv(k_norm[1], normed.at[pl.ds(128, 32)], below)
+    recv(k_norm[2], normed.at[pl.ds(224, 32)], above)
+    recv(k_norm[3], normed.at[pl.ds(160, 32)], below)
+    kv_near()
+
+    q_str.on(2)
+    q_str.on(3)
     o_str.wait_a()
     o_str.first(0)
     o_str.first(1)
+    q_rows(1, slot)
+
+    @pl.when(jnp.logical_not(takes))
+    def _():
+        recv(k_an_in[0], an_mine, pair)
+
+    for d in (1, 3, 2):
+        recv(k_an_in[d], an_one(core, b, (a + 4 - d) % 4), pair)
+    an_gather.send_b()
     q_str.last(0)
     q_str.last(1)
+    q_str.last(2)
+    q_str.last(3)
     an_gather.wait_b()
     q_str.wait_d()
+    o_str.on(0)
     q_rows(1, other)
+    o_str.on(1)
     an_gather.wait_d()
 
     @pl.when(t != 1)
@@ -550,8 +578,6 @@
     send_sum(0)
     o_str.wait_d((0,))
     send_sum(1)
-    o_str.on(0)
-    o_str.on(1)
     send_sum(2)
     send_sum(3)
     o_str.wait_d((1, 3))
@@ -591,7 +617,7 @@
 
     @pl.when(takes)
     def _():
-        for i in range(3):
+        for i in range(15):
             anchor_copy(i).wait_send()
 
     @pl.when(t <= 2)
@@ -634,7 +660,7 @@
         angle = np.asarray(positions, np.float64)[:, None] * np.concatenate([freq, freq])[None]
         return np.cos(angle).astype(np.float32), (np.sin(angle) * sign).astype(np.float32)
 
-    return (*both(np.arange(128) * 512), *both(np.arange(512)))
+    return np.stack(both(np.concatenate([np.arange(512), np.arange(128) * 512])))
 
 
 def body(hidden_in, norm_gain, w_query, w_key, w_value, w_out, offsets):
@@ -643,7 +669,7 @@
     return pl.pallas_call(
         kernel,
         out_shape=jax.ShapeDtypeStruct((128, 4096), BF16),
-        in_specs=[pl.BlockSpec(memory_space=pltpu.SMEM)] + [vmem] * 6 + [hbm] * 4,
+        in_specs=[pl.BlockSpec(memory_space=pltpu.SMEM), vmem] + [hbm] * 6,
         out_specs=vmem,
         scratch_shapes=[
             pltpu.VMEM((2, 8, 512, 512), BF16),
@@ -663,13 +689,15 @@
             pltpu.VMEM((128, 4096), F32),
             pltpu.VMEM((272, 128), F32),
             pltpu.VMEM((272, 128), F32),
+            pltpu.VMEM((128, 4096), BF16),
+            pltpu.VMEM((2, 640, 128), F32),
             pltpu.SemaphoreType.DMA((N_SEM,)),
             pltpu.SemaphoreType.DMA((N_SEM,)),
-            pltpu.SemaphoreType.DMA((19,)),
+            pltpu.SemaphoreType.DMA((21,)),
         ],
         compiler_params=pltpu.CompilerParams(collective_id=0, has_side_effects=True, vmem_limit_bytes=56 * 2**20),
         cost_estimate=pl.CostEstimate(flops=10**10, bytes_accessed=2 * 10**7, transcendentals=2 * 10**6),
-    )(offsets, hidden_in, norm_gain.reshape(1, 4096), *angle_tables(), w_query, w_key, w_value, w_out)
+    )(offsets, norm_gain.reshape(1, 4096), hidden_in, angle_tables(), w_query, w_key, w_value, w_out)
 
 
 def solution(mesh):

time: 80 us -> 73.9 us (0.924)
  Pallas kernels: 77.5 us -> 71.4 us
    pallas_call x1, Pallas kernels: 77.5 us -> 71.4 us  [body(): pl.pallas_call(kernel, out_shape=jax.ShapeDtypeStruct((128, 4096), BF16),...]
where the time goes in v3:
time: 73.9 us; the launch traced here: 73.7 us
  Pallas kernels  71.4 us (97%)
  local copies, waits for them, and re-layouts  2.29 us (3%)
    pallas_call x1, Pallas kernels, body(): pl.pallas_call(kernel, out_shape=jax.ShapeDtypeStruct((128, 4096), BF16),...  71.4 us
    unnamed x1, local copies, waits for them, and re-layouts  2.29 us

profile of v3, /device:TPU:1, one launch (start us, length us, event | category | flops | bytes accessed | tf_op | source)
XLA Modules:
  0.0 73.7 jit_solution(6099685174129176811)
XLA Ops:
  0.0 71.4 %shard_map.82 = bf16[128,4096]{1,0:T(8,128)(2,1)} custom-call(s32[64]{0:T(128)} %offsets_ref.1, f32[1,4096]{1,0:T(1,128)} %bitcast.1, bf16[128,4096]{1,0:T(8,128)(2,1)} %x_hbm.1, f32[2,640,128]{2,1,0:T(8,128)} %constant.2.clone.tables_hbm, bf16[4096,512]{1,0:T(8,128)(2,1)} %wq_hbm.1, bf16[4096,128]{1,0:T(8,128)(2,1)} %wk_hbm.1, bf16[4096,128]{1,0:T(8,128)(2,1)} %wv_hbm.1, ...), custom_call_target="tpu_custom_call" | custom-call | flops 10000000000 | bytes 20000000 | tf_op jit(solution)/shard_map/pallas_call | solution.py:669
  71.4 2.3 %copy.10 = bf16[128,4096]{1,0:T(8,128)(2,1)} copy(bf16[128,4096]{1,0:T(8,128)(2,1)} %shard_map.82) | data formatting | bytes 2097152

commit v4 on v3

--- a/solution.py
+++ b/solution.py
@@ -9,6 +9,7 @@
 HD = 128
 EPS = 1e-05
 NEG = -1e30
+LOG2_E = 1.4426950408889634
 MESH = pl.DeviceIdType.MESH
 F32 = jnp.float32
 BF16 = jnp.bfloat16
@@ -18,7 +19,7 @@
 def kernel(
     offsets_ref, gain_ref, x_hbm, tables_hbm, wq_hbm, wk_hbm, wv_hbm, wo_hbm, out_ref,
     w_q, w_kv, w_o, normed, grain, grain_norm, anchor_kv, block_kv, q_own, q_near, att_own, att_near, send_buf, recv_buf,
-    partial, cos_ref, sin_ref, x_ref, tables_ref, ss, rs, ls,
+    partial, cos_ref, sin_ref, x_ref, tables_ref, out_buf, ss, rs, ls,
 ):
     ctx = lax.axis_index("context")
     t = lax.axis_index("tensor")
@@ -534,7 +535,7 @@
     v = kv_view(low_foreign, both, (high_start + 256) % 512, 64)
     recv(k_high, v, along_z(6))
 
-    scale = 1.0 / HD**0.5
+    scale = LOG2_E / HD**0.5
     dims = (((1,), (1,)), ((), ()))
 
     def attend(q, i, buf, block, start, length):
@@ -542,11 +543,11 @@
         s2 = lax.dot_general(q, block_kv[buf, i, :, pl.ds(0, 128)], dims, preferred_element_type=F32)
         qpos = start + lax.broadcasted_iota(jnp.int32, (256, 512), 0) % length
         kpos = lax.broadcasted_iota(jnp.int32, (256, 512), 1)
-        s1 = jnp.where(block == 0, NEG, s1 * scale)
-        s2 = jnp.where(kpos <= qpos, s2 * scale, NEG)
-        top = jnp.maximum(jnp.max(s1, axis=-1, keepdims=True), jnp.max(s2, axis=-1, keepdims=True))
-        e1 = jnp.exp(s1 - top)
-        e2 = jnp.exp(s2 - top)
+        s2 = jnp.where(kpos <= qpos, s2, NEG)
+        hidden = jnp.where(block == 0, NEG, 0.0)
+        top = jnp.maximum(jnp.max(s1, axis=-1, keepdims=True) + hidden, jnp.max(s2, axis=-1, keepdims=True))
+        e1 = jnp.exp2((s1 - (top - hidden)) * scale)
+        e2 = jnp.exp2((s2 - top) * scale)
         total = jnp.sum(e1, axis=-1, keepdims=True) + jnp.sum(e2, axis=-1, keepdims=True)
         o = jnp.dot(e1.astype(BF16), anchor_kv[i, :, pl.ds(128, 128)], preferred_element_type=F32)
         o += jnp.dot(e2.astype(BF16), block_kv[buf, i, :, pl.ds(128, 128)], preferred_element_type=F32)
@@ -642,11 +643,17 @@
 
     for cp in sends[:-16]:
         cp.wait_send()
+    stores = []
     for i in range(8):
         recv(k_sum[i][0], recv_buf.at[i, upper], above)
         recv(k_sum[i][1], recv_buf.at[i, lower], below)
         cols = pl.ds(pl.multiple_of(order[i] * 512, 512), 512)
-        out_ref[:, cols] = (partial[:, cols] + recv_buf[i].astype(F32)).astype(BF16)
+        out_buf[i] = (partial[:, cols] + recv_buf[i].astype(F32)).astype(BF16)
+        cp = pltpu.make_async_copy(out_buf.at[i], out_ref.at[:, cols], ls.at[i])
+        cp.start()
+        stores.append(cp)
+    for cp in stores:
+        cp.wait()
     for cp in sends[-16:]:
         cp.wait_send()
     assert count[0] <= N_SEM, count[0]
@@ -670,7 +677,7 @@
         kernel,
         out_shape=jax.ShapeDtypeStruct((128, 4096), BF16),
         in_specs=[pl.BlockSpec(memory_space=pltpu.SMEM), vmem] + [hbm] * 6,
-        out_specs=vmem,
+        out_specs=hbm,
         scratch_shapes=[
             pltpu.VMEM((2, 8, 512, 512), BF16),
             pltpu.VMEM((2, 4096, 256), BF16),
@@ -691,6 +698,7 @@
             pltpu.VMEM((272, 128), F32),
             pltpu.VMEM((128, 4096), BF16),
             pltpu.VMEM((2, 640, 128), F32),
+            pltpu.VMEM((8, 128, 512), BF16),
             pltpu.SemaphoreType.DMA((N_SEM,)),
             pltpu.SemaphoreType.DMA((N_SEM,)),
             pltpu.SemaphoreType.DMA((21,)),

time: 73.9 us -> 73.5 us (level)
  no operation moved by 1% of the time
where the time goes in v4:
time: 73.5 us; the launch traced here: 73.3 us
  Pallas kernels  71 us (97%)
  local copies, waits for them, and re-layouts  2.29 us (3%)
    pallas_call x1, Pallas kernels, body(): pl.pallas_call(kernel, out_shape=jax.ShapeDtypeStruct((128, 4096), BF16),...  71 us
    unnamed x1, local copies, waits for them, and re-layouts  2.29 us

profile of v4, /device:TPU:1, one launch (start us, length us, event | category | flops | bytes accessed | tf_op | source)
XLA Modules:
  0.0 73.3 jit_solution(1804888253741578856)
XLA Ops:
  0.0 71.0 %shard_map.82 = bf16[128,4096]{1,0:T(8,128)(2,1)} custom-call(s32[64]{0:T(128)} %offsets_ref.1, f32[1,4096]{1,0:T(1,128)} %bitcast.1, bf16[128,4096]{1,0:T(8,128)(2,1)} %x_hbm.1, f32[2,640,128]{2,1,0:T(8,128)} %constant.2.clone.tables_hbm, bf16[4096,512]{1,0:T(8,128)(2,1)} %wq_hbm.1, bf16[4096,128]{1,0:T(8,128)(2,1)} %wk_hbm.1, bf16[4096,128]{1,0:T(8,128)(2,1)} %wv_hbm.1, ...), custom_call_target="tpu_custom_call" | custom-call | flops 10000000000 | bytes 20000000 | tf_op jit(solution)/shard_map/pallas_call | solution.py:676
  71.0 2.3 %copy.10 = bf16[128,4096]{1,0:T(8,128)(2,1)} copy(bf16[128,4096]{1,0:T(8,128)(2,1)} %shard_map.82) | data formatting | bytes 2097152
